TPU v7x, 512 devices: a whole 4x8x8 slice. The times are simulated.
512 devices in a mesh: blk: 16 (over x_lo, y), lane: 32 (over x_hi, z, core).
Axes of the slice: x: 4 (x_hi: 2, x_lo: 2; x = x_hi * 2 + x_lo), y: 8, z: 8, core: 2. Of those that a mesh axis runs over, the one named last changes fastest.
Arguments:
- incident: bfloat16 [16, 4096, 128], P('blk', 'lane'), may hold values from -6 to 6
- geometry: float32 [16, 6, 4096], P('blk', None, 'lane'), may hold values from -30 to 30, as said below
- order: int32 [16, 32, 128], P('blk', 'lane'), may hold values from 0 to 127, each once within a row
- pairs: int32 [16, 32, 2, 192], P('blk', 'lane'), may hold values from 0 to 63, as said below
- counts: int32 [16, 32], P('blk', 'lane'), may hold values from 48 to 192, as said below
Outputs:
- currents: float32 [16, 4096, 128], P('blk', 'lane')
Inputs may be any that keep to these rules, and one draw needn't show every extreme that they name: `geometry`: positions and area vectors of facets; area vectors are far smaller than positions. For each device (b, l) the entries i < counts[b, l] are distinct visible pairs, ordered by target block (row 1) non-decreasing; row 0 lies in 0 to 5; entries from counts[b, l] on are in range and carry no interaction. `counts`: some device has all 192 pairs visible.
All inputs are finite; a program needn't handle non-finite values.
Results may differ from a plain program's by a relative error of at most 0.00035.
Values sent between devices are 32-bit elements; how exact they have to be, the bound alone decides.
A program may use at most 64 MiB of HBM per device.

v0:
```python
import math

import jax
import jax.numpy as jnp
from jax import lax
from jax.sharding import PartitionSpec as P

BS = 64
FB = 2


def extended(shard, sides, width):
    for axis, dim in sides:
        size, length = (lax.axis_size(axis), shard.shape[dim])
        up = [(i, (i + 1) % size) for i in range(size)]
        down = [(j, i) for i, j in up]
        last = lax.slice_in_dim(shard, length - width, length, axis=dim)
        first = lax.slice_in_dim(shard, 0, width, axis=dim)
        before = lax.ppermute(last, axis, up)
        after = lax.ppermute(first, axis, down)
        shard = jnp.concatenate([before, shard, after], axis=dim)
    return shard


def passed_along(block, axis, distance):
    devices = range(lax.axis_size(axis))
    route = [((i - distance) % len(devices), i) for i in devices]
    return lax.ppermute(block, axis, route)


def green_block(target, source):
    width = source.shape[-1]
    tiled = jnp.concatenate([source, source], axis=-1)
    offset = tiled[:, :, None, :] - target[:3, :, :, None]
    radius = jnp.sqrt(jnp.sum(offset * offset, axis=0) + 1.0)
    facing = jnp.sum(target[3:, :, :, None] * offset, axis=0) / (radius * radius)
    phase = jnp.where(jnp.arange(2 * width) >= width, 0.5 * math.pi, 0.0)
    return facing * jnp.cos(2.0 * math.pi * radius + phase)


def apply_block(green, current):
    half = current.shape[-1] // 2
    turned = jnp.concatenate([-current[..., half:], current[..., :half]], axis=-1)
    stacked = jnp.concatenate([current, turned], axis=1)
    return jnp.einsum(
        "gik,gkc->gic",
        green,
        stacked,
        precision=lax.Precision.HIGHEST,
        preferred_element_type=jnp.float32,
    )


def per_device(incident, geometry, order, pairs, counts):
    local_order = order[0, 0]
    facets = local_order.shape[0]
    lanes = lax.axis_size("lane")
    width = incident.shape[2]
    group = 16
    own_geo = jnp.take(geometry[0], local_order, axis=1)
    target_geo = lax.all_gather(own_geo, "lane", axis=1, tiled=True).reshape(6, lanes * FB, BS)
    source_geo = extended(own_geo[:3], (("blk", 1),), facets)
    source_geo = source_geo.reshape(3, 3 * FB, BS)
    start = jnp.take(incident[0], local_order, axis=0)
    pair_list = pairs[0, 0]
    capacity = pair_list.shape[1]
    live_count = counts[0, 0]
    padded = jnp.concatenate([pair_list, jnp.zeros((2, group), jnp.int32)], axis=1)
    valid = jnp.arange(capacity, dtype=jnp.int32) < live_count
    target_index = pair_list[1]

    def block_field(window, first_block, blocks):
        first_pair = jnp.sum(valid & (target_index < first_block))
        last_pair = jnp.sum(valid & (target_index < first_block + blocks))
        window_blocks = window.reshape(3 * FB, BS, width)

        def group_term(index, total):
            begin = first_pair + index * group
            piece = lax.dynamic_slice_in_dim(padded, begin, group, 1)
            live = begin + jnp.arange(group, dtype=jnp.int32) < last_pair
            green = green_block(
                jnp.take(target_geo, piece[1], axis=1), jnp.take(source_geo, piece[0], axis=1)
            )
            contrib = apply_block(green, jnp.take(window_blocks, piece[0], axis=0))
            placed = jnp.where(live, piece[1] - first_block, blocks)
            return total.at[placed].add(contrib, mode="drop")

        turns = (last_pair - first_pair + group - 1) // group
        zero = jnp.zeros((blocks, BS, width), jnp.float32)
        return lax.fori_loop(0, turns, group_term, zero).reshape(blocks * BS, width)

    def neighbours(current):
        lower = passed_along(current, "blk", 1)
        upper = passed_along(current, "blk", -1)
        window = jnp.concatenate([lower, current, upper], axis=0)
        return window

    def lane_field(window):
        result = lax.psum_scatter(
            block_field(window, 0, lanes * FB), "lane", scatter_dimension=0, tiled=True
        )
        return result

    base = start.astype(jnp.float32)
    current = base
    current = base + lane_field(neighbours(current))
    final = base + lane_field(neighbours(current))
    return jnp.zeros_like(final).at[local_order].set(final)[None]


def solution(mesh):
    placed = (
        P("blk", "lane", None),
        P("blk", None, "lane"),
        P("blk", "lane", None),
        P("blk", "lane", None, None),
        P("blk", "lane"),
    )
    return jax.shard_map(
        per_device, mesh=mesh, in_specs=placed, out_specs=P("blk", "lane", None), check_vma=False
    )
```

profile of v0, /device:TPU:1, one launch (start us, length us, event | category | flops | bytes accessed | tf_op | source)
XLA Modules:
  0.0 592.2 jit_solution(8779458304653041822)
XLA Ops:
  7.9 0.8 copy.42
  9.4 6.9 %collective-permute-start.1 = (f32[3,128]{0,1:T(8,128)S(1)}, f32[3,128]{0,1:T(8,128)S(1)}, u32[]{:S(2)}, u32[]{:S(2)}) collective-permute-start(f32[3,128]{0,1:T(8,128)S(1)} %bitcast.75), channel_id=1, source_target_pairs={{32,0},{64,32},{96,64},{128,96},{160,128},{192,160},{224,192},{256... | collective-permute-start | bytes 4616 | tf_op jit(solution)/shard_map/ppermute | solution.py:20
  16.3 1.9 collective-permute-start
  18.2 0.7 gather_fusion.6
  19.0 5.5 collective-permute-start.3
  24.5 1.9 collective-permute-start.2
  27.1 0.7 compare_reduce_fusion
  27.8 0.7 fusion.50
  28.5 55.0 %all_gather.3 = f32[6,4096]{0,1:T(8,128)S(1)} all-gather(f32[6,128]{0,1:T(8,128)S(1)} %select_bitcast_fusion.4), channel_id=1, replica_groups=mesh['blk'=16,'lane'=32] {'lane'}, dimensions={1}, use_global_device_ids=true | all-gather | bytes 101376 | tf_op jit(solution)/shard_map/all_gather | solution.py:61
  84.9 1.4 copy.48
  86.8 51.0 %while.20 = (s32[]{:T(128)}, f32[64,64,128]{2,1,0:T(8,128)S(1)}, s32[]{:T(128)}, s32[]{:T(128)}, s32[]{:T(128)}, /*index=5*/s32[2,208]{1,0:T(2,128)S(1)}, f32[6,...) while((s32[]{:T(128)}, f32[64,64,128]{2,1,0:T(8,128)S(1)}, ...), condition=%wide.region_6.10_spmd, body=%wide.region_2.9_spmd.sunk | while | flops 204686880 | bytes 8780051 | solution.py:90
  89.0 1.5 gather_fusion.1
  91.4 1.0 fusion.72
  92.6 3.1 fusion.73
  95.7 1.3 scatter_fusion
  99.2 1.5 gather_fusion.1
  101.6 1.0 fusion.72
  102.8 3.1 fusion.73
  105.9 1.3 scatter_fusion
  107.9 0.7 fusion.70
  109.4 1.5 gather_fusion.1
  111.7 1.0 fusion.72
  113.0 3.1 fusion.73
  116.1 1.3 scatter_fusion
  118.1 0.7 fusion.70
  119.6 1.5 gather_fusion.1
  122.0 1.0 fusion.72
  123.2 3.1 fusion.73
  126.3 1.3 scatter_fusion
  129.8 1.5 gather_fusion.1
  132.2 1.0 fusion.72
  133.4 3.1 fusion.73
  136.5 1.3 scatter_fusion
  137.9 1.3 copy-done.1
  139.3 185.5 %reduce-scatter.3.cloned.1.call-done = f32[128,128]{1,0:T(8,128)} async-done(((f32[4096,128]{1,0:T(8,128)}), f32[128,128]{1,0:T(8,128)}) %reduce-scatter.3.cloned.1.call-update) | async-done | bytes 65552 | tf_op jit(solution)/shard_map/reduce_scatter | solution.py:99
  324.8 0.9 convert_add_fusion
  325.7 4.3 collective-permute-start.5
  330.0 1.9 collective-permute-start.4
  331.9 5.2 collective-permute-done.4
  337.4 51.2 %while.21 = (s32[]{:T(128)}, f32[64,64,128]{2,1,0:T(8,128)S(1)}, s32[]{:T(128)}, s32[]{:T(128)}, s32[]{:T(128)}, /*index=5*/s32[2,208]{1,0:T(2,128)S(1)}, f32[6,...) while((s32[]{:T(128)}, f32[64,64,128]{2,1,0:T(8,128)S(1)}, ...), condition=%wide.region_12.16_spmd, body=%wide.region_8.15_spmd.sunk | while | flops 204686880 | bytes 8780051 | solution.py:90
  338.2 0.7 fusion.76
  339.8 1.5 gather_fusion.4
  342.1 1.0 fusion.78
  343.4 3.1 fusion.79
  346.4 1.3 scatter_fusion.1
  350.0 1.5 gather_fusion.4
  352.3 1.0 fusion.78
  353.6 3.1 fusion.79
  356.6 1.3 scatter_fusion.1
  360.1 1.5 gather_fusion.4
  362.5 1.0 fusion.78
  363.8 3.1 fusion.79
  366.8 1.3 scatter_fusion.1
  370.4 1.5 gather_fusion.4
  372.7 1.0 fusion.78
  374.0 3.1 fusion.79
  377.0 1.3 scatter_fusion.1
  380.6 1.5 gather_fusion.4
  382.9 1.0 fusion.78
  384.2 3.1 fusion.79
  387.2 1.3 scatter_fusion.1
  388.6 1.3 copy-done.2
  390.0 193.6 %reduce-scatter.5.cloned.1.call-done = f32[128,128]{1,0:T(8,128)} async-done(((f32[4096,128]{1,0:T(8,128)}), f32[128,128]{1,0:T(8,128)}) %reduce-scatter.5.cloned.1.call-update) | async-done | bytes 65552 | tf_op jit(solution)/shard_map/reduce_scatter | solution.py:99
  583.6 1.8 scatter_custom_fusion.2
  (189 shorter events, 26.4 us)
Async XLA Ops:
  6.5 11.7 %copy-start = (bf16[1,128,128]{2,1,0:T(8,128)(2,1)S(1)}, bf16[1,128,128]{2,1,0:T(8,128)(2,1)}, u32[]{:S(2)}) copy-start(bf16[1,128,128]{2,1,0:T(8,128)(2,1)} %param.15) | copy-start | bytes 98308
  6.5 78.3 %copy-start.3 = (s32[1,1,2,192]{3,2,1,0:T(2,128)S(1)}, s32[1,1,2,192]{3,2,1,0:T(2,128)}, u32[]{:S(2)}) copy-start(s32[1,1,2,192]{3,2,1,0:T(2,128)} %param.18) | copy-start | bytes 4612
  6.5 318.2 %reduce-scatter.3.cloned.1.call-start = ((), (), s32[]{:S(2)}) async-start(), calls=%async_computation.2 | async-start | bytes 2162688 | tf_op jit(solution)/shard_map/reduce_scatter | solution.py:99
  9.4 76.9 %collective-permute-start.1 = (f32[3,128]{0,1:T(8,128)S(1)}, f32[3,128]{0,1:T(8,128)S(1)}, u32[]{:S(2)}, u32[]{:S(2)}) collective-permute-start(f32[3,128]{0,1:T(8,128)S(1)} %bitcast.75), channel_id=1, source_target_pairs={{32,0},{64,32},{96,64},{128,96},{160,128},{192,160},{224,192},{256... | collective-permute-start | bytes 4616 | tf_op jit(solution)/shard_map/ppermute | solution.py:20
  16.3 70.1 %collective-permute-start = (f32[3,128]{0,1:T(8,128)S(1)}, f32[3,128]{0,1:T(8,128)S(1)}, u32[]{:S(2)}, u32[]{:S(2)}) collective-permute-start(f32[3,128]{0,1:T(8,128)S(1)} %bitcast.76), channel_id=1, source_target_pairs={{0,32},{32,64},{64,96},{96,128},{128,160},{160,192},{192,224},{224... | collective-permute-start | bytes 4616 | tf_op jit(solution)/shard_map/ppermute | solution.py:19
  19.0 67.5 %collective-permute-start.3 = (f32[128,128]{1,0:T(8,128)S(1)}, f32[128,128]{1,0:T(8,128)S(1)}, u32[]{:S(2)}, u32[]{:S(2)}) collective-permute-start(f32[128,128]{1,0:T(8,128)S(1)} %fusion.53), channel_id=1, source_target_pairs={{32,0},{64,32},{96,64},{128,96},{160,128},{192,160},{224,192},{256... | collective-permute-start | bytes 196616 | tf_op jit(solution)/shard_map/ppermute | solution.py:28
  24.5 62.1 %collective-permute-start.2 = (f32[128,128]{1,0:T(8,128)S(1)}, f32[128,128]{1,0:T(8,128)S(1)}, u32[]{:S(2)}, u32[]{:S(2)}) collective-permute-start(f32[128,128]{1,0:T(8,128)S(1)} %fusion.53), channel_id=1, source_target_pairs={{480,0},{0,32},{32,64},{64,96},{96,128},{128,160},{160,192},{192,2... | collective-permute-start | bytes 196616 | tf_op jit(solution)/shard_map/ppermute | solution.py:28
  137.9 1.4 copy-start.1
  139.2 444.3 %reduce-scatter.5.cloned.1.call-start = ((), (), s32[]{:S(2)}) async-start(), calls=%async_computation.3 | async-start | bytes 2162688 | tf_op jit(solution)/shard_map/reduce_scatter | solution.py:99
  325.7 6.3 %collective-permute-start.5 = (f32[128,128]{1,0:T(8,128)S(1)}, f32[128,128]{1,0:T(8,128)S(1)}, u32[]{:S(2)}, u32[]{:S(2)}) collective-permute-start(f32[128,128]{1,0:T(8,128)S(1)} %convert_add_fusion), channel_id=1, source_target_pairs={{32,0},{64,32},{96,64},{128,96},{160,128},{192,160},{224,192},{256... | collective-permute-start | bytes 196616 | tf_op jit(solution)/shard_map/ppermute | solution.py:28
  330.0 7.1 %collective-permute-start.4 = (f32[128,128]{1,0:T(8,128)S(1)}, f32[128,128]{1,0:T(8,128)S(1)}, u32[]{:S(2)}, u32[]{:S(2)}) collective-permute-start(f32[128,128]{1,0:T(8,128)S(1)} %convert_add_fusion), channel_id=1, source_target_pairs={{480,0},{0,32},{32,64},{64,96},{96,128},{128,160},{160,192},{192,2... | collective-permute-start | bytes 196616 | tf_op jit(solution)/shard_map/ppermute | solution.py:28
  388.6 1.4 copy-start.2
Sparse Core Ops, SparseCore 0:
  139.4 185.3 reduce-scatter.2
  390.1 193.4 reduce-scatter.4
where the time goes:
time: 598 us; the launch traced here: 592 us
  waiting for transfers between devices  384 us (64%)
  blocking collectives  55 us (9%)
  other arithmetic  42.1 us (7%)
  local copies, waits for them, and re-layouts  34.9 us (6%)
  matrix products  30.7 us (5%)
  starting transfers between devices  22.4 us (4%)
  between operations  15.5 us (3%)
  loops' own time  7.35 us (1%)
    reduce_scatter x2, waiting for transfers between devices, lane_field(): lax.psum_scatter(block_field(window, 0, lanes * FB), 'lane', scatter_dime...  379 us
    all_gather x1, blocking collectives, per_device(): lax.all_gather(own_geo, 'lane', axis=1, tiled=True)  55 us
    dot_general x10, matrix products, apply_block(): jnp.einsum('gik,gkc->gic', green, stacked, precision=lax.Precision.HIGHES...  30.7 us
    gather x10, local copies, waits for them, and re-layouts, group_term(): jnp.take(target_geo, piece[1], axis=1)  15.1 us
    ppermute x4, starting transfers between devices, passed_along(): return lax.ppermute(block, axis, route)  13.6 us
    scatter-add x10, other arithmetic, group_term(): return total.at[placed].add(contrib, mode='drop')  13.4 us
  transfers between devices with their start and end apart: 8, of which 3 were waited for; matrix products, arithmetic and copies ran while one was open for 1% of the time, Pallas kernels for 0%

commit v1 on v0

v1 whole, which is shorter than its diff:
```python
import functools

import jax
import jax.numpy as jnp
from jax import lax
from jax.experimental import pallas as pl
from jax.experimental.pallas import tpu as pltpu
from jax.sharding import PartitionSpec as P

BS = 64
FB = 2
FPD = BS * FB
COLS = 128
INFO = 16
LIST = 256
PMAX = 192
CYC = 3
ROWS = CYC * 2 * FPD

F32 = jnp.float32
BF16 = jnp.bfloat16
MESH = pl.DeviceIdType.MESH
ROUND = 12582912.0
SIN = (4.442867903016683, -7.307443420820961, 3.5947880748152716, -0.7843740225385425)
COS = (
    -1.4142134965649493,
    6.978850988230643,
    -5.7394611705151934,
    1.8835629862356886,
    -0.3106981896782719,
)


def split(value):
    high = value.astype(BF16)
    return high, (value - high.astype(F32)).astype(BF16)


def split3(value):
    high, low = split(value)
    rest = value - high.astype(F32) - low.astype(F32)
    return high, low, rest.astype(BF16)


def dot(a, b):
    return jnp.dot(a, b, preferred_element_type=F32)


def kernel(
    nb,
    nz,
    inc_ref,
    geo_ref,
    order_ref,
    pairs_ref,
    count_ref,
    out_ref,
    geo_in,
    target,
    first,
    second,
    mask,
    weight,
    green_hi,
    green_lo,
    total,
    part_in,
    geo_send,
    geo_recv,
    half_send,
    half_recv,
    ring_send,
    ring_recv,
    part_send,
    part_recv,
):
    blk = lax.axis_index("blk")
    lane = lax.axis_index("lane")
    core = lane % 2
    chip = lane // 2
    z = chip % nz
    x_hi = chip // nz
    reach = nz // 2
    sibling = lane + 1 - 2 * core
    across = (1 - x_hi) * (2 * nz) + z * 2 + core
    right = x_hi * (2 * nz) + ((z + 1) % nz) * 2 + core
    left = x_hi * (2 * nz) + ((z + nz - 1) % nz) * 2 + core

    def cycle(c):
        return (blk + (c - 1) + nb) % nb

    owners = [
        (c, e, (cycle(c), lane if e == 0 else sibling))
        for c, e in ((0, 0), (2, 0), (0, 1), (2, 1), (1, 1))
    ]
    near = [(blk, across), (blk, right), (blk, left)]

    barrier = pltpu.get_barrier_semaphore()
    for device in [d for _, _, d in owners] + near:
        pl.semaphore_signal(barrier, inc=1, device_id=device, device_id_type=MESH)

    facet = lax.broadcasted_iota(jnp.int32, (FPD, FPD), 0)
    placed = jnp.where(order_ref[...] == facet, 1.0, 0.0).astype(F32)
    placed16 = placed.astype(BF16)
    picked16 = jnp.transpose(placed).astype(BF16)
    start = dot(picked16, inc_ref[...])
    first[0, 0:FPD, :] = start
    first[0, FPD : FPD + INFO, :] = jnp.zeros((INFO, COLS), F32)
    geo_in[2] = jnp.full((8, LIST), -1.0, F32)
    pieces = split3(geo_ref[...])
    geo_in[2, 0:6, 0:FPD] = sum(dot(piece, placed16) for piece in pieces)
    live = lax.broadcasted_iota(jnp.int32, (2, PMAX), 1) < count_ref[...]
    geo_in[2, 6:8, 0:PMAX] = jnp.where(live, pairs_ref[...], -1).astype(F32)

    pl.semaphore_wait(barrier, len(owners) + len(near))

    sends = []

    def copy(source, dest, send, recv, device):
        return pltpu.make_async_remote_copy(
            src_ref=source,
            dst_ref=dest,
            send_sem=send,
            recv_sem=recv,
            device_id=device,
            device_id_type=MESH,
        )

    def put(*args):
        made = copy(*args)
        made.start()
        sends.append(made)

    for c, e, device in owners:
        mine = (2 - c) * 2 + e
        put(geo_in.at[2], geo_in.at[mine], geo_send.at[mine], geo_recv.at[mine], device)

    def spread(slot):
        turned = jnp.transpose(geo_in[slot, :, 0:FPD])
        for row in range(6):
            target[row, slot * FPD : (slot + 1) * FPD, :] = jnp.broadcast_to(
                turned[:, row : row + 1], (FPD, FPD)
            )

    total[...] = jnp.zeros(total.shape, F32)
    spread(2)
    for c, e, device in owners:
        slot = c * 2 + e
        copy(
            geo_in.at[2], geo_in.at[slot], geo_send.at[slot], geo_recv.at[slot], device
        ).wait_recv()
        spread(slot)
    for c in range(CYC):
        for row in range(2):
            base = FPD + row * 6 + c * 2
            first[0, base : base + 1, :] = geo_in[c * 2, 6 + row : 7 + row, 0:128]
            first[0, base + 1 : base + 2, :] = geo_in[c * 2, 6 + row : 7 + row, 128:256]
    first[0, FPD + 12 : FPD + 15, :] = geo_in[2, 0:3, 0:FPD]

    def ring_sem(sweep, way, h, d):
        return ((sweep * 2 + way) * 2 + h) * reach + d

    def ring_copy(sweep, buf, way, h, d):
        if way == 0:
            here, there, device = (nz - d) % nz, nz - d - 1, (blk, right)
        else:
            here, there, device = d, d + 1, (blk, left)
        height = buf.shape[1]
        rows = pl.ds(0, height)
        if d == reach - 1:
            rows = pl.ds(way * (height // 2), height // 2)
        sem = ring_sem(sweep, way, h, d)
        return (
            buf.at[h * nz + here, rows],
            buf.at[h * nz + there, rows],
            ring_send.at[sem],
            ring_recv.at[sem],
            device,
        )

    def gather(sweep, buf, work):
        def forward(h, d):
            for way in range(2):
                put(*ring_copy(sweep, buf, way, h, d))

        def arrive(h, d):
            for way in range(2):
                copy(*ring_copy(sweep, buf, way, h, d)).wait_recv()

        cross = (buf.at[0], buf.at[nz], half_send.at[sweep], half_recv.at[sweep], (blk, across))
        put(*cross)
        forward(0, 0)
        work(0, 1, 1)
        copy(*cross).wait_recv()
        forward(1, 0)
        work(nz, 1, 1)
        for d in range(1, reach):
            for h in range(2):
                arrive(h, d - 1)
                forward(h, d)
                work(h * nz + d, nz - 2 * d, 2)
        for h in range(2):
            arrive(h, reach - 1)
        work(reach, nz, 2)

    lane_half = lax.broadcasted_iota(jnp.int32, (INFO, COLS), 1) // BS
    wanted_row = lax.broadcasted_iota(jnp.int32, (INFO, COLS), 0)
    wanted_part = wanted_row % 4
    wanted = (2 * (2 * chip + (core + wanted_part // 2) % 2) + wanted_part % 2).astype(F32)
    wanted = [jnp.where(wanted_row // 4 == c, wanted, -5.0) for c in range(CYC)]
    sign = jnp.where(lax.broadcasted_iota(jnp.int32, (FPD, COLS), 1) < BS, -1.0, 1.0)

    def stacked(current):
        swapped = jnp.concatenate([current[:, BS:], current[:, :BS]], axis=1)
        return current, swapped * sign

    def visible(slot):
        seen = [jnp.zeros((INFO, COLS), F32), jnp.zeros((INFO, COLS), F32)]
        info = first[slot, FPD : FPD + INFO, :]
        for row in range(2 * CYC):
            c = row // 2
            hit = info[6 + row : 7 + row, :] == wanted[c]
            for side in range(2):
                same = info[row : row + 1, :] == float(2 * (2 - c) + side)
                seen[side] += jnp.where(hit & same, 1.0, 0.0)
        sums = [jnp.sum(s, axis=1, keepdims=True) for s in seen]
        mask[...] = jnp.where(lane_half == 0, sums[0], sums[1])

    def green_work(base, stride, count):
        def one(j, _):
            slot = base + j * stride
            upper, lower = stacked(first[slot, 0:FPD, :])
            weight[0:FPD, 0:COLS] = upper.astype(BF16)
            weight[FPD : 2 * FPD, 0:COLS] = lower.astype(BF16)
            visible(slot)

            def chunk(i, _):
                rows = pl.ds(pl.multiple_of(i * FPD, FPD), FPD)
                place = first[slot, FPD + 12 : FPD + 15, :]
                offset = [place[k : k + 1, :] - target[k, rows, :] for k in range(3)]
                square = offset[0] * offset[0] + offset[1] * offset[1]
                square = square + offset[2] * offset[2] + 1.0
                inverse = lax.rsqrt(square)
                radius = square * inverse
                facing = sum(target[3 + k, rows, :] * offset[k] for k in range(3))
                shown = mask[pl.ds(2 * i, 2), :]
                shown = jnp.concatenate(
                    [jnp.broadcast_to(shown[k : k + 1, :], (BS, COLS)) for k in range(FB)], axis=0
                )
                facing = facing * shown * (inverse * inverse)
                turn = radius - ((radius + ROUND) - ROUND)
                power = turn * turn
                sine = turn * (((SIN[3] * power + SIN[2]) * power + SIN[1]) * power + SIN[0])
                cosine = COS[4] * power + COS[3]
                cosine = ((cosine * power + COS[2]) * power + COS[1]) * power + COS[0]
                real_hi, real_lo = split(facing * (1.0 - sine * sine))
                imag_hi, imag_lo = split(facing * (sine * cosine))
                high = jnp.concatenate([real_hi, imag_hi], axis=1)
                low = jnp.concatenate([real_lo, imag_lo], axis=1)
                green_hi[slot, rows, :] = high
                green_lo[slot, rows, :] = low
                term = dot(jnp.concatenate([high, low], axis=0), weight[:, 0:COLS])
                total[0, rows, :] += term[0:FPD] + term[FPD : 2 * FPD]
                return 0

            lax.fori_loop(0, 2 * CYC, chunk, 0)
            return 0

        lax.fori_loop(0, count, one, 0)

    def field_work(base, stride, count):
        def one(j, _):
            slot = base + j * stride
            for half, value in enumerate(stacked(second[slot])):
                high, low = split(value)
                weight[half * FPD : (half + 1) * FPD, 0:COLS] = high
                weight[half * FPD : (half + 1) * FPD, COLS : 2 * COLS] = low

            def chunk(i, _):
                rows = pl.ds(pl.multiple_of(i * 2 * FPD, 2 * FPD), 2 * FPD)
                term = dot(green_hi[slot, rows, :], weight[...])
                rest = dot(green_lo[slot, rows, :], weight[:, 0:COLS])
                total[1, rows, :] += term[:, 0:COLS] + (term[:, COLS:] + rest)
                return 0

            lax.fori_loop(0, CYC, chunk, 0)
            return 0

        lax.fori_loop(0, count, one, 0)

    def exchange(sweep):
        def args(c, e, device):
            index = (0, 1, None, 2, 3, 4)[(2 - c) * 2 + e]
            return (
                total.at[sweep, pl.ds((c * 2 + e) * FPD, FPD)],
                part_in.at[sweep, index],
                part_send.at[sweep * 5 + index],
                part_recv.at[sweep * 5 + index],
                device,
            )

        for c, e, device in owners:
            put(*args(c, e, device))
        result = start + total[sweep, 2 * FPD : 3 * FPD, :]
        for c, e, device in owners:
            copy(*args(c, e, device)).wait_recv()
        for index in range(5):
            result = result + part_in[sweep, index]
        return result

    gather(0, first, green_work)
    second[0] = exchange(0)
    gather(1, second, field_work)
    final = exchange(1)
    out_ref[...] = sum(dot(placed16, piece) for piece in split3(final))

    for made in sends:
        made.wait_send()


def per_device(incident, geometry, order, pairs, counts):
    nb = lax.axis_size("blk")
    nz = lax.axis_size("lane") // 4
    reach = nz // 2
    vmem = pl.BlockSpec(memory_space=pltpu.VMEM)
    out = pl.pallas_call(
        functools.partial(kernel, nb, nz),
        out_shape=jax.ShapeDtypeStruct((FPD, COLS), F32),
        in_specs=[vmem] * 5,
        out_specs=vmem,
        scratch_shapes=[
            pltpu.VMEM((2 * CYC, 8, LIST), F32),
            pltpu.VMEM((6, ROWS, FPD), F32),
            pltpu.VMEM((2 * nz, FPD + INFO, COLS), F32),
            pltpu.VMEM((2 * nz, FPD, COLS), F32),
            pltpu.VMEM((INFO, COLS), F32),
            pltpu.VMEM((2 * FPD, 2 * COLS), BF16),
            pltpu.VMEM((2 * nz, ROWS, 2 * FPD), BF16),
            pltpu.VMEM((2 * nz, ROWS, 2 * FPD), BF16),
            pltpu.VMEM((2, ROWS, COLS), F32),
            pltpu.VMEM((2, 5, FPD, COLS), F32),
            pltpu.SemaphoreType.DMA((6,)),
            pltpu.SemaphoreType.DMA((6,)),
            pltpu.SemaphoreType.DMA((2,)),
            pltpu.SemaphoreType.DMA((2,)),
            pltpu.SemaphoreType.DMA((8 * reach,)),
            pltpu.SemaphoreType.DMA((8 * reach,)),
            pltpu.SemaphoreType.DMA((10,)),
            pltpu.SemaphoreType.DMA((10,)),
        ],
        compiler_params=pltpu.CompilerParams(
            collective_id=0, has_side_effects=True, vmem_limit_bytes=40 * 2**20
        ),
        name="sweeps",
    )(incident[0], geometry[0], order[0], pairs[0, 0], counts)
    return out[None]


def solution(mesh):
    placed = (
        P("blk", "lane", None),
        P("blk", None, "lane"),
        P("blk", "lane", None),
        P("blk", "lane", None, None),
        P("blk", "lane"),
    )
    return jax.shard_map(
        per_device, mesh=mesh, in_specs=placed, out_specs=P("blk", "lane", None), check_vma=False
    )
```

time: 598 us -> 83.9 us (0.14)
  waiting for transfers between devices: 384 us -> 0 us
  Pallas kernels: 0 us -> 79.8 us
  blocking collectives: 55 us -> 0 us
  other arithmetic: 42.1 us -> 0 us
  local copies, waits for them, and re-layouts: 34.9 us -> 2.75 us
  matrix products: 30.7 us -> 0 us
  starting transfers between devices: 22.4 us -> 0 us
  between operations: 15.5 us -> 0.67 us
  loops' own time: 7.35 us -> 0 us
    reduce_scatter x2 -> x0, waiting for transfers between devices: 379 us -> none  [lane_field(): lax.psum_scatter(block_field(window, 0, lanes * FB), 'lane', scatter_dime...]
    pallas_call x0 -> x1, Pallas kernels: none -> 79.8 us  [per_device(): pl.pallas_call(functools.partial(kernel, nb, nz), out_shape=jax.ShapeDtyp...]
    all_gather x1 -> x0, blocking collectives: 55 us -> none  [per_device(): lax.all_gather(own_geo, 'lane', axis=1, tiled=True)]
    dot_general x10 -> x0, matrix products: 30.7 us -> none  [apply_block(): jnp.einsum('gik,gkc->gic', green, stacked, precision=lax.Precision.HIGHES...]
    gather x32 -> x0, local copies, waits for them, and re-layouts: 28.1 us -> none  [the longest x10 15.1 us: group_term(): jnp.take(target_geo, piece[1], axis=1)]
    ppermute x6 -> x0, starting transfers between devices: 22.4 us -> none  [the longest x4 13.6 us: passed_along(): return lax.ppermute(block, axis, route)]
    scatter-add x10 -> x0, other arithmetic: 13.4 us -> none  [group_term(): return total.at[placed].add(contrib, mode='drop')]
    reduce_sum x11 -> x0, other arithmetic: 11.1 us -> none  [the longest x10 10.4 us: green_block(): radius = jnp.sqrt(jnp.sum(offset * offset, axis=0) + 1.0)]
  transfers between devices with their start and end apart: 8 -> 0, of which waited for: 3 -> 0; matrix products, arithmetic and copies ran while one was open for 1% -> 0% of each run, Pallas kernels for 0% -> 0%
where the time goes in v1:
time: 83.9 us; the launch traced here: 83.2 us
  Pallas kernels  79.8 us (95%)
  local copies, waits for them, and re-layouts  2.75 us (3%)
    pallas_call x1, Pallas kernels, per_device(): pl.pallas_call(functools.partial(kernel, nb, nz), out_shape=jax.ShapeDtyp...  79.8 us
    unnamed x10, local copies, waits for them, and re-layouts  2.75 us

profile of v1, /device:TPU:1, one launch (start us, length us, event | category | flops | bytes accessed | tf_op | source)
XLA Modules:
  0.0 83.2 jit_solution(16474088150148687058)
XLA Ops:
  0.7 0.0 copy-start.3
  0.7 0.7 copy-done.3
  1.3 0.0 copy-start.1
  1.3 0.0 copy-start.2
  1.3 0.7 copy-done.1
  2.0 0.0 copy-done.2
  2.0 0.0 copy-start
  2.0 0.8 copy-done
  2.8 79.8 %sweeps.1 = f32[128,128]{1,0:T(8,128)S(1)} custom-call(bf16[128,128]{1,0:T(8,128)(2,1)S(1)} %bitcast.8, f32[6,128]{1,0:T(8,128)S(1)} %bitcast.9, s32[1,128]{1,0:T(1,128)S(1)} %bitcast.11, s32[2,192]{1,0:T(2,128)S(1)} %bitcast.10, s32[1,1]{1,0:T(1,128)S(6)} %copy.10.count_ref), custom_call_target="tpu_custom_call" | custom-call | tf_op jit(solution)/shard_map/sweeps/pallas_call | solution.py:326
  82.6 0.6 copy.11
  (1 shorter events, 0.0 us)
Async XLA Ops:
  0.7 0.7 copy-start.3
  1.3 0.7 copy-start.1
  1.3 0.7 copy-start.2
  2.0 0.8 copy-start

commit v2 on v1

v2 whole, which is shorter than its diff:
```python
import functools

import jax
import jax.numpy as jnp
from jax import lax
from jax.experimental import pallas as pl
from jax.experimental.pallas import tpu as pltpu
from jax.sharding import PartitionSpec as P

BS = 64
FB = 2
FPD = BS * FB
COLS = 128
INFO = 16
LIST = 256
PMAX = 192
CYC = 3
ROWS = CYC * 2 * FPD

F32 = jnp.float32
BF16 = jnp.bfloat16
MESH = pl.DeviceIdType.MESH
ROUND = 12582912.0
SIN = (4.442867903016683, -7.307443420820961, 3.5947880748152716, -0.7843740225385425)
COS = (
    -1.4142134965649493,
    6.978850988230643,
    -5.7394611705151934,
    1.8835629862356886,
    -0.3106981896782719,
)


def split(value):
    high = value.astype(BF16)
    return high, (value - high.astype(F32)).astype(BF16)


def split3(value):
    high, low = split(value)
    rest = value - high.astype(F32) - low.astype(F32)
    return high, low, rest.astype(BF16)


def dot(a, b):
    return jnp.dot(a, b, preferred_element_type=F32)


def kernel(
    nb,
    nz,
    inc_ref,
    geo_ref,
    order_ref,
    pairs_ref,
    count_ref,
    out_ref,
    geo_in,
    target,
    current,
    info,
    mask,
    weight,
    green_hi,
    green_lo,
    total,
    part_in,
    geo_send,
    geo_recv,
    info_send,
    info_recv,
    ring_send,
    ring_recv,
    part_send,
    part_recv,
):
    blk = lax.axis_index("blk")
    lane = lax.axis_index("lane")
    core = lane % 2
    chip = lane // 2
    z = chip % nz
    x_hi = chip // nz
    sibling = lane + 1 - 2 * core
    across = (blk, (1 - x_hi) * (2 * nz) + z * 2 + core)

    def along(step):
        return (blk, x_hi * (2 * nz) + ((z + step + nz) % nz) * 2 + core)

    def cycle(c):
        return (blk + (c - 1) + nb) % nb

    owners = [
        (c, e, (cycle(c), lane if e == 0 else sibling))
        for c, e in ((0, 0), (2, 0), (0, 1), (2, 1), (1, 1))
    ]
    near = [across, along(1), along(-1), along(2), along(-2)]

    barrier = pltpu.get_barrier_semaphore()
    for device in [d for _, _, d in owners] + near:
        pl.semaphore_signal(barrier, inc=1, device_id=device, device_id_type=MESH)

    facet = lax.broadcasted_iota(jnp.int32, (FPD, FPD), 0)
    placed = jnp.where(order_ref[...] == facet, 1.0, 0.0).astype(F32)
    placed16 = placed.astype(BF16)
    picked16 = jnp.transpose(placed).astype(BF16)
    start = dot(picked16, inc_ref[...])
    current[0, 0] = start
    info[0] = jnp.zeros((INFO, COLS), F32)
    geo_in[2] = jnp.full((8, LIST), -1.0, F32)
    pieces = split3(geo_ref[...])
    geo_in[2, 0:6, 0:FPD] = sum(dot(piece, placed16) for piece in pieces)
    live = lax.broadcasted_iota(jnp.int32, (2, PMAX), 1) < count_ref[...]
    geo_in[2, 6:8, 0:PMAX] = jnp.where(live, pairs_ref[...], -1).astype(F32)

    pl.semaphore_wait(barrier, len(owners) + len(near))

    sends = []

    def copy(source, dest, send, recv, device):
        return pltpu.make_async_remote_copy(
            src_ref=source,
            dst_ref=dest,
            send_sem=send,
            recv_sem=recv,
            device_id=device,
            device_id_type=MESH,
        )

    def put(place, *which):
        copy(*place(*which)).start()
        sends.append((place, which))

    def slot_of(h, d):
        return h * nz + d % nz

    full, top, bottom = (pl.ds(0, FPD), pl.ds(0, FPD // 2), pl.ds(FPD // 2, FPD // 2))
    hops = [
        ((0, 0), (0, -2), full, along(2)),
        ((0, 0), (0, 2), full, along(-2)),
        ((0, 0), (0, -1), full, along(1)),
        ((0, 0), (0, 1), full, along(-1)),
        ((0, 0), (1, 0), full, across),
        ((0, -2), (0, -3), full, along(1)),
        ((0, 2), (0, 3), full, along(-1)),
        ((0, -2), (0, 4), top, along(2)),
        ((0, 2), (0, 4), bottom, along(-2)),
        ((0, -2), (1, -2), full, across),
        ((0, 2), (1, 2), full, across),
        ((0, -1), (1, -1), full, across),
        ((0, 1), (1, 1), full, across),
        ((1, -2), (1, -3), full, along(1)),
        ((1, 2), (1, 3), full, along(-1)),
        ((0, 4), (1, 4), full, across),
    ]

    def hop(sweep, k):
        source, dest, rows, device = hops[k]
        return (
            current.at[sweep, slot_of(*source), rows],
            current.at[sweep, slot_of(*dest), rows],
            ring_send.at[sweep * len(hops) + k],
            ring_recv.at[sweep * len(hops) + k],
            device,
        )

    def pass_on(sweep, *which):
        for k in which:
            put(hop, sweep, k)

    def arrive(sweep, *which):
        for k in which:
            copy(*hop(sweep, k)).wait_recv()

    def note(source, dest, device):
        there = slot_of(*dest)
        return (
            info.at[slot_of(*source)],
            info.at[there],
            info_send.at[there],
            info_recv.at[there],
            device,
        )

    def tell(*steps):
        for step in steps:
            put(note, (0, 0), (0, -step), along(step))

    def told(h, *distances):
        for d in distances:
            if h == 0:
                copy(*note((0, 0), (0, d), along(-d))).wait_recv()
                put(note, (0, d), (1, d), across)
            else:
                copy(*note((0, d), (1, d), across)).wait_recv()

    def place_of(slot, device):
        return geo_in.at[2], geo_in.at[slot], geo_send.at[slot], geo_recv.at[slot], device

    for c, e, device in owners:
        put(place_of, (2 - c) * 2 + e, device)
    pass_on(0, 0, 1, 2, 3, 4)

    def spread(slot):
        turned = jnp.transpose(geo_in[slot, :, 0:FPD])
        for row in range(6):
            target[row, slot * FPD : (slot + 1) * FPD, :] = jnp.broadcast_to(
                turned[:, row : row + 1], (FPD, FPD)
            )

    total[...] = jnp.zeros(total.shape, F32)
    spread(2)
    for c, e, device in owners:
        copy(*place_of(c * 2 + e, device)).wait_recv()
    for c in range(CYC):
        for row in range(2):
            base = row * 6 + c * 2
            info[0, base : base + 1, :] = geo_in[c * 2, 6 + row : 7 + row, 0:128]
            info[0, base + 1 : base + 2, :] = geo_in[c * 2, 6 + row : 7 + row, 128:256]
    info[0, 12:15, :] = geo_in[2, 0:3, 0:FPD]
    tell(1, -1, 2, -2)
    put(note, (0, 0), (1, 0), across)

    lane_half = lax.broadcasted_iota(jnp.int32, (INFO, COLS), 1) // BS
    wanted_row = lax.broadcasted_iota(jnp.int32, (INFO, COLS), 0)
    wanted_part = wanted_row % 4
    wanted = (2 * (2 * chip + (core + wanted_part // 2) % 2) + wanted_part % 2).astype(F32)
    wanted = [jnp.where(wanted_row // 4 == c, wanted, -5.0) for c in range(CYC)]
    sign = jnp.where(lax.broadcasted_iota(jnp.int32, (FPD, COLS), 1) < BS, -1.0, 1.0)

    def stacked(value):
        swapped = jnp.concatenate([value[:, BS:], value[:, :BS]], axis=1)
        return value, swapped * sign

    def visible(slot):
        seen = [jnp.zeros((INFO, COLS), F32), jnp.zeros((INFO, COLS), F32)]
        told_rows = info[slot]
        for row in range(2 * CYC):
            c = row // 2
            hit = told_rows[6 + row : 7 + row, :] == wanted[c]
            for side in range(2):
                same = told_rows[row : row + 1, :] == float(2 * (2 - c) + side)
                seen[side] += jnp.where(hit & same, 1.0, 0.0)
        sums = [jnp.sum(s, axis=1, keepdims=True) for s in seen]
        mask[...] = jnp.where(lane_half == 0, sums[0], sums[1])

    def make_green(slot, i):
        place = info[slot, 12:15, :]
        for part in range(2 * FB):
            rows = pl.ds(pl.multiple_of((i * 2 * FB + part) * BS, BS), BS)
            offset = [place[k : k + 1, :] - target[k, rows, :] for k in range(3)]
            square = offset[0] * offset[0] + offset[1] * offset[1]
            square = square + offset[2] * offset[2] + 1.0
            inverse = lax.rsqrt(square)
            radius = square * inverse
            facing = sum(target[3 + k, rows, :] * offset[k] for k in range(3))
            facing = facing * mask[pl.ds(2 * FB * i + part, 1), :] * (inverse * inverse)
            turn = radius - ((radius + ROUND) - ROUND)
            power = turn * turn
            sine = turn * (((SIN[3] * power + SIN[2]) * power + SIN[1]) * power + SIN[0])
            cosine = COS[4] * power + COS[3]
            cosine = ((cosine * power + COS[2]) * power + COS[1]) * power + COS[0]
            pieces = split(facing * (1.0 - sine * sine)), split(facing * (sine * cosine))
            for half in range(2):
                lanes = pl.ds(half * FPD, FPD)
                green_hi[slot, rows, lanes], green_lo[slot, rows, lanes] = pieces[half]

    def weigh_start(slot):
        for half, value in enumerate(stacked(current[0, slot])):
            weight[half * FPD : (half + 1) * FPD, 0:COLS] = value.astype(BF16)

    def add_start(slot, i):
        rows = pl.ds(pl.multiple_of(i * 2 * FPD, 2 * FPD), 2 * FPD)
        both = jnp.concatenate([green_hi[slot, rows, :], green_lo[slot, rows, :]], axis=0)
        term = dot(both, weight[:, 0:COLS])
        total[0, rows, :] += term[0 : 2 * FPD] + term[2 * FPD :]

    def add_swept(slot):
        for half, value in enumerate(stacked(current[1, slot])):
            high, low = split(value)
            weight[half * FPD : (half + 1) * FPD, 0:COLS] = high
            weight[half * FPD : (half + 1) * FPD, COLS : 2 * COLS] = low
        term = dot(green_hi[slot], weight[...])
        rest = dot(green_lo[slot], weight[:, 0:COLS])
        total[1] += term[:, 0:COLS] + (term[:, COLS:] + rest)

    def picked(order, n):
        return sum(jnp.int32(n == k) * slot_of(*place) for k, place in enumerate(order))

    def chunks(body):
        def one(i, _):
            body(i)
            return 0

        lax.fori_loop(0, CYC, one, 0)

    def partial_of(sweep, c, e, device):
        index = (0, 1, None, 2, 3, 4)[(2 - c) * 2 + e]
        return (
            total.at[sweep, pl.ds((c * 2 + e) * FPD, FPD)],
            part_in.at[sweep, index],
            part_send.at[sweep * 5 + index],
            part_recv.at[sweep * 5 + index],
            device,
        )

    def exchange(sweep):
        for owner in owners:
            put(partial_of, sweep, *owner)
        result = start + total[sweep, 2 * FPD : 3 * FPD, :]
        for owner in owners:
            copy(*partial_of(sweep, *owner)).wait_recv()
        for index in range(5):
            result = result + part_in[sweep, index]
        return result

    arrive(0, 0, 1)
    pass_on(0, 5, 6, 7, 8, 9, 10)
    arrive(0, 2, 3)
    pass_on(0, 11, 12)
    tell(3, -3, 4)
    for slot in (0, 1, 3, 4, 5):
        spread(slot)

    order = [(0, 0), (0, -1), (0, 1), (0, -2), (0, 2), (0, -3), (0, 3), (0, 4)]
    order += [(1, 0), (1, -1), (1, 1), (1, -2), (1, 2), (1, -3), (1, 3), (1, 4)]

    def start_step(n, _):
        @pl.when(n == 1)
        def _():
            told(0, -1, 1)

        @pl.when(n == 3)
        def _():
            told(0, -2, 2)
            arrive(0, 9, 10)
            pass_on(0, 13, 14)

        @pl.when(n == 4)
        def _():
            arrive(0, 7, 8)
            pass_on(0, 15)

        @pl.when(n == 5)
        def _():
            told(0, -3, 3, 4)
            arrive(0, 5, 6)

        @pl.when(n == 8)
        def _():
            told(1, 0)
            arrive(0, 4)

        @pl.when(n == 9)
        def _():
            told(1, -1, 1)
            arrive(0, 11, 12)

        @pl.when(n == 11)
        def _():
            told(1, -2, 2)

        @pl.when(n == 13)
        def _():
            told(1, -3, 3)
            arrive(0, 13, 14)

        @pl.when(n == 15)
        def _():
            told(1, 4)

        slot = picked(order, n)
        prior = picked(order, n - 1)
        weigh_start(prior)
        visible(slot)

        def both(i):
            add_start(prior, i)
            make_green(slot, i)

        chunks(both)
        return 0

    visible(0)
    chunks(functools.partial(make_green, 0))
    lax.fori_loop(1, 2 * nz, start_step, 0)
    arrive(0, 15)
    weigh_start(slot_of(1, 4))
    chunks(functools.partial(add_start, slot_of(1, 4)))

    swept = [(0, 0), (0, -1), (0, 1), (0, -2), (0, 2), (1, 0), (1, -1), (1, 1)]
    swept += [(0, -3), (0, 3), (1, -2), (1, 2), (0, 4), (1, -3), (1, 3), (1, 4)]

    def swept_step(n, _):
        @pl.when(n == 1)
        def _():
            arrive(1, 2, 3)
            pass_on(1, 11, 12)
            arrive(1, 0, 1)
            pass_on(1, 5, 6, 7, 8, 9, 10)

        @pl.when(n == 5)
        def _():
            arrive(1, 4)

        @pl.when(n == 6)
        def _():
            arrive(1, 9, 10)
            pass_on(1, 13, 14)
            arrive(1, 7, 8)
            pass_on(1, 15)
            arrive(1, 11, 12)

        @pl.when(n == 8)
        def _():
            arrive(1, 5, 6)

        @pl.when(n == 13)
        def _():
            arrive(1, 13, 14)

        @pl.when(n == 15)
        def _():
            arrive(1, 15)

        add_swept(picked(swept, n))
        return 0

    current[1, 0] = exchange(0)
    pass_on(1, 0, 1, 2, 3, 4)
    lax.fori_loop(0, 2 * nz, swept_step, 0)
    final = exchange(1)
    out_ref[...] = sum(dot(placed16, piece) for piece in split3(final))

    for place, which in sends:
        copy(*place(*which)).wait_send()


def per_device(incident, geometry, order, pairs, counts):
    nb = lax.axis_size("blk")
    nz = lax.axis_size("lane") // 4
    vmem = pl.BlockSpec(memory_space=pltpu.VMEM)
    out = pl.pallas_call(
        functools.partial(kernel, nb, nz),
        out_shape=jax.ShapeDtypeStruct((FPD, COLS), F32),
        in_specs=[vmem] * 5,
        out_specs=vmem,
        scratch_shapes=[
            pltpu.VMEM((2 * CYC, 8, LIST), F32),
            pltpu.VMEM((6, ROWS, FPD), F32),
            pltpu.VMEM((2, 2 * nz, FPD, COLS), F32),
            pltpu.VMEM((2 * nz, INFO, COLS), F32),
            pltpu.VMEM((INFO, COLS), F32),
            pltpu.VMEM((2 * FPD, 2 * COLS), BF16),
            pltpu.VMEM((2 * nz, ROWS, 2 * FPD), BF16),
            pltpu.VMEM((2 * nz, ROWS, 2 * FPD), BF16),
            pltpu.VMEM((2, ROWS, COLS), F32),
            pltpu.VMEM((2, 5, FPD, COLS), F32),
            pltpu.SemaphoreType.DMA((6,)),
            pltpu.SemaphoreType.DMA((6,)),
            pltpu.SemaphoreType.DMA((2 * nz,)),
            pltpu.SemaphoreType.DMA((2 * nz,)),
            pltpu.SemaphoreType.DMA((32,)),
            pltpu.SemaphoreType.DMA((32,)),
            pltpu.SemaphoreType.DMA((10,)),
            pltpu.SemaphoreType.DMA((10,)),
        ],
        compiler_params=pltpu.CompilerParams(
            collective_id=0, has_side_effects=True, vmem_limit_bytes=40 * 2**20
        ),
        name="sweeps",
    )(incident[0], geometry[0], order[0], pairs[0, 0], counts)
    return out[None]


def solution(mesh):
    placed = (
        P("blk", "lane", None),
        P("blk", None, "lane"),
        P("blk", "lane", None),
        P("blk", "lane", None, None),
        P("blk", "lane"),
    )
    return jax.shard_map(
        per_device, mesh=mesh, in_specs=placed, out_specs=P("blk", "lane", None), check_vma=False
    )
```

time: 83.9 us -> 75.7 us (0.902)
  Pallas kernels: 79.8 us -> 72 us
    pallas_call x1, Pallas kernels: 79.8 us -> 72 us  [per_device(): pl.pallas_call(functools.partial(kernel, nb, nz), out_shape=jax.ShapeDtyp...]
where the time goes in v2:
time: 75.7 us; the launch traced here: 75.4 us
  Pallas kernels  72 us (95%)
  local copies, waits for them, and re-layouts  2.75 us (4%)
    pallas_call x1, Pallas kernels, per_device(): pl.pallas_call(functools.partial(kernel, nb, nz), out_shape=jax.ShapeDtyp...  72 us
    unnamed x10, local copies, waits for them, and re-layouts  2.75 us

profile of v2, /device:TPU:1, one launch (start us, length us, event | category | flops | bytes accessed | tf_op | source)
XLA Modules:
  0.0 75.4 jit_solution(3782547021351485248)
XLA Ops:
  0.7 0.0 copy-start.3
  0.7 0.7 copy-done.3
  1.3 0.0 copy-start.1
  1.3 0.0 copy-start.2
  1.3 0.7 copy-done.1
  2.0 0.0 copy-done.2
  2.0 0.0 copy-start
  2.0 0.8 %copy-done = bf16[1,128,128]{2,1,0:T(8,128)(2,1)S(1)} copy-done((bf16[1,128,128]{2,1,0:T(8,128)(2,1)S(1)}, bf16[1,128,128]{2,1,0:T(8,128)(2,1)}, u32[]{:S(2)}) %copy-start) | copy-done | bytes 32792
  2.8 72.0 %sweeps.1 = f32[128,128]{1,0:T(8,128)S(1)} custom-call(bf16[128,128]{1,0:T(8,128)(2,1)S(1)} %bitcast.8, f32[6,128]{1,0:T(8,128)S(1)} %bitcast.9, s32[1,128]{1,0:T(1,128)S(1)} %bitcast.11, s32[2,192]{1,0:T(2,128)S(1)} %bitcast.10, s32[1,1]{1,0:T(1,128)S(6)} %copy.10.count_ref), custom_call_target="tpu_custom_call" | custom-call | tf_op jit(solution)/shard_map/sweeps/pallas_call | solution.py:442
  74.8 0.6 copy.11
  (1 shorter events, 0.0 us)
Async XLA Ops:
  0.7 0.7 copy-start.3
  1.3 0.7 copy-start.1
  1.3 0.7 copy-start.2
  2.0 0.8 %copy-start = (bf16[1,128,128]{2,1,0:T(8,128)(2,1)S(1)}, bf16[1,128,128]{2,1,0:T(8,128)(2,1)}, u32[]{:S(2)}) copy-start(bf16[1,128,128]{2,1,0:T(8,128)(2,1)} %param.5) | copy-start | bytes 98308

commit v3 on v2

--- a/solution.py
+++ b/solution.py
@@ -83,8 +83,13 @@
     sibling = lane + 1 - 2 * core
     across = (blk, (1 - x_hi) * (2 * nz) + z * 2 + core)
 
+    steps = {
+        step: (blk, x_hi * (2 * nz) + ((z + step + nz) % nz) * 2 + core)
+        for step in (1, -1, 2, -2, 3, -3, 4)
+    }
+
     def along(step):
-        return (blk, x_hi * (2 * nz) + ((z + step + nz) % nz) * 2 + core)
+        return steps[step]
 
     def cycle(c):
         return (blk + (c - 1) + nb) % nb
@@ -130,10 +135,13 @@
         copy(*place(*which)).start()
         sends.append((place, which))
 
+    slots = [(0, 0), (0, -1), (0, 1), (0, -2), (0, 2), (1, 0), (1, -1), (1, 1)]
+    slots += [(1, -2), (1, 2), (0, -3), (0, 3), (0, 4), (1, -3), (1, 3), (1, 4)]
+
     def slot_of(h, d):
-        return h * nz + d % nz
-
-    full, top, bottom = (pl.ds(0, FPD), pl.ds(0, FPD // 2), pl.ds(FPD // 2, FPD // 2))
+        return slots.index((h, 4 if d == -4 else d))
+
+    full, top, bottom = (0, FPD), (0, FPD // 2), (FPD // 2, FPD // 2)
     hops = [
         ((0, 0), (0, -2), full, along(2)),
         ((0, 0), (0, 2), full, along(-2)),
@@ -153,13 +161,23 @@
         ((0, 4), (1, 4), full, across),
     ]
 
+    halves = []
+    for source, dest, (base, height), device in hops:
+        for part in range(2):
+            rows = (base + part * height // 2, height // 2)
+            halves.append((source, dest, rows, device))
+
+    def half(part, *which):
+        return [2 * k + part for k in which]
+
     def hop(sweep, k):
-        source, dest, rows, device = hops[k]
+        source, dest, rows, device = (hops, halves)[sweep][k]
+        sem = sweep * len(hops) + k
         return (
-            current.at[sweep, slot_of(*source), rows],
-            current.at[sweep, slot_of(*dest), rows],
-            ring_send.at[sweep * len(hops) + k],
-            ring_recv.at[sweep * len(hops) + k],
+            current.at[sweep, slot_of(*source), pl.ds(*rows)],
+            current.at[sweep, slot_of(*dest), pl.ds(*rows)],
+            ring_send.at[sem],
+            ring_recv.at[sem],
             device,
         )
 
@@ -188,7 +206,7 @@
     def told(h, *distances):
         for d in distances:
             if h == 0:
-                copy(*note((0, 0), (0, d), along(-d))).wait_recv()
+                copy(*note((0, 0), (0, d), across)).wait_recv()
                 put(note, (0, d), (1, d), across)
             else:
                 copy(*note((0, d), (1, d), across)).wait_recv()
@@ -283,9 +301,6 @@
         rest = dot(green_lo[slot], weight[:, 0:COLS])
         total[1] += term[:, 0:COLS] + (term[:, COLS:] + rest)
 
-    def picked(order, n):
-        return sum(jnp.int32(n == k) * slot_of(*place) for k, place in enumerate(order))
-
     def chunks(body):
         def one(i, _):
             body(i)
@@ -313,63 +328,71 @@
             result = result + part_in[sweep, index]
         return result
 
-    arrive(0, 0, 1)
-    pass_on(0, 5, 6, 7, 8, 9, 10)
-    arrive(0, 2, 3)
-    pass_on(0, 11, 12)
-    tell(3, -3, 4)
     for slot in (0, 1, 3, 4, 5):
         spread(slot)
 
-    order = [(0, 0), (0, -1), (0, 1), (0, -2), (0, 2), (0, -3), (0, 3), (0, 4)]
-    order += [(1, 0), (1, -1), (1, 1), (1, -2), (1, 2), (1, -3), (1, 3), (1, 4)]
-
-    def start_step(n, _):
-        @pl.when(n == 1)
+    def start_step(slot, _):
+        @pl.when(slot == 1)
         def _():
             told(0, -1, 1)
 
-        @pl.when(n == 3)
-        def _():
+        @pl.when(slot == 2)
+        def _():
+            arrive(0, 2, 3)
+            pass_on(0, 11, 12)
+
+        @pl.when(slot == 3)
+        def _():
+            arrive(0, 0, 1)
+            tell(3, -3, 4)
             told(0, -2, 2)
+            pass_on(0, 5, 6, 9, 10, 7, 8)
+
+        @pl.when(slot == 5)
+        def _():
+            told(1, 0)
+
+        @pl.when(slot == 6)
+        def _():
+            told(1, -1, 1)
+            arrive(0, 4)
+
+        @pl.when(slot == 7)
+        def _():
+            arrive(0, 11, 12)
+
+        @pl.when(slot == 8)
+        def _():
+            told(1, -2, 2)
             arrive(0, 9, 10)
             pass_on(0, 13, 14)
 
-        @pl.when(n == 4)
+        @pl.when(slot == 9)
+        def _():
+            told(0, -3, 3, 4)
+
+        @pl.when(slot == 10)
         def _():
             arrive(0, 7, 8)
             pass_on(0, 15)
 
-        @pl.when(n == 5)
-        def _():
-            told(0, -3, 3, 4)
+        @pl.when(slot == 11)
+        def _():
             arrive(0, 5, 6)
 
-        @pl.when(n == 8)
-        def _():
-            told(1, 0)
-            arrive(0, 4)
-
-        @pl.when(n == 9)
-        def _():
-            told(1, -1, 1)
-            arrive(0, 11, 12)
-
-        @pl.when(n == 11)
-        def _():
-            told(1, -2, 2)
-
-        @pl.when(n == 13)
+        @pl.when(slot == 13)
         def _():
             told(1, -3, 3)
+
+        @pl.when(slot == 14)
+        def _():
             arrive(0, 13, 14)
 
-        @pl.when(n == 15)
+        @pl.when(slot == 15)
         def _():
             told(1, 4)
 
-        slot = picked(order, n)
-        prior = picked(order, n - 1)
+        prior = slot - 1
         weigh_start(prior)
         visible(slot)
 
@@ -387,46 +410,46 @@
     weigh_start(slot_of(1, 4))
     chunks(functools.partial(add_start, slot_of(1, 4)))
 
-    swept = [(0, 0), (0, -1), (0, 1), (0, -2), (0, 2), (1, 0), (1, -1), (1, 1)]
-    swept += [(0, -3), (0, 3), (1, -2), (1, 2), (0, 4), (1, -3), (1, 3), (1, 4)]
-
     def swept_step(n, _):
         @pl.when(n == 1)
         def _():
-            arrive(1, 2, 3)
-            pass_on(1, 11, 12)
-            arrive(1, 0, 1)
-            pass_on(1, 5, 6, 7, 8, 9, 10)
+            for part in range(2):
+                arrive(1, *half(part, 0, 1))
+                pass_on(1, *half(part, 5, 6, 9, 10), *half(0, 7 + part), *half(1, 7 + part))
+                arrive(1, *half(part, 2, 3))
+                pass_on(1, *half(part, 11, 12))
 
         @pl.when(n == 5)
         def _():
-            arrive(1, 4)
+            arrive(1, *half(0, 4), *half(1, 4))
 
         @pl.when(n == 6)
         def _():
-            arrive(1, 9, 10)
-            pass_on(1, 13, 14)
-            arrive(1, 7, 8)
-            pass_on(1, 15)
-            arrive(1, 11, 12)
-
-        @pl.when(n == 8)
-        def _():
-            arrive(1, 5, 6)
+            for part in range(2):
+                arrive(1, *half(part, 9, 10))
+                pass_on(1, *half(part, 13, 14))
+            arrive(1, *half(0, 7, 8), *half(1, 7, 8))
+            pass_on(1, *half(0, 15), *half(1, 15))
+            arrive(1, *half(0, 11, 12), *half(1, 11, 12))
+
+        @pl.when(n == 10)
+        def _():
+            arrive(1, *half(0, 5, 6), *half(1, 5, 6))
 
         @pl.when(n == 13)
         def _():
-            arrive(1, 13, 14)
+            arrive(1, *half(0, 13, 14), *half(1, 13, 14))
 
         @pl.when(n == 15)
         def _():
-            arrive(1, 15)
-
-        add_swept(picked(swept, n))
+            arrive(1, *half(0, 15), *half(1, 15))
+
+        add_swept(n)
         return 0
 
     current[1, 0] = exchange(0)
-    pass_on(1, 0, 1, 2, 3, 4)
+    for part in range(2):
+        pass_on(1, *half(part, 0, 1, 2, 3, 4))
     lax.fori_loop(0, 2 * nz, swept_step, 0)
     final = exchange(1)
     out_ref[...] = sum(dot(placed16, piece) for piece in split3(final))
@@ -459,8 +482,8 @@
             pltpu.SemaphoreType.DMA((6,)),
             pltpu.SemaphoreType.DMA((2 * nz,)),
             pltpu.SemaphoreType.DMA((2 * nz,)),
-            pltpu.SemaphoreType.DMA((32,)),
-            pltpu.SemaphoreType.DMA((32,)),
+            pltpu.SemaphoreType.DMA((48,)),
+            pltpu.SemaphoreType.DMA((48,)),
             pltpu.SemaphoreType.DMA((10,)),
             pltpu.SemaphoreType.DMA((10,)),
         ],

time: 75.7 us -> 70.7 us (0.934)
  Pallas kernels: 72 us -> 67.1 us
    pallas_call x1, Pallas kernels: 72 us -> 67.1 us  [per_device(): pl.pallas_call(functools.partial(kernel, nb, nz), out_shape=jax.ShapeDtyp...]
where the time goes in v3:
time: 70.7 us; the launch traced here: 70.5 us
  Pallas kernels  67.1 us (95%)
  local copies, waits for them, and re-layouts  2.75 us (4%)
    pallas_call x1, Pallas kernels, per_device(): pl.pallas_call(functools.partial(kernel, nb, nz), out_shape=jax.ShapeDtyp...  67.1 us
    unnamed x10, local copies, waits for them, and re-layouts  2.75 us

profile of v3, /device:TPU:1, one launch (start us, length us, event | category | flops | bytes accessed | tf_op | source)
XLA Modules:
  0.0 70.5 jit_solution(616600200790565936)
XLA Ops:
  0.7 0.0 copy-start.3
  0.7 0.7 copy-done.3
  1.3 0.0 copy-start.1
  1.3 0.0 copy-start.2
  1.3 0.7 copy-done.1
  2.0 0.0 copy-done.2
  2.0 0.0 copy-start
  2.0 0.8 %copy-done = bf16[1,128,128]{2,1,0:T(8,128)(2,1)S(1)} copy-done((bf16[1,128,128]{2,1,0:T(8,128)(2,1)S(1)}, bf16[1,128,128]{2,1,0:T(8,128)(2,1)}, u32[]{:S(2)}) %copy-start) | copy-done | bytes 32792
  2.8 67.1 %sweeps.1 = f32[128,128]{1,0:T(8,128)S(1)} custom-call(bf16[128,128]{1,0:T(8,128)(2,1)S(1)} %bitcast.8, f32[6,128]{1,0:T(8,128)S(1)} %bitcast.9, s32[1,128]{1,0:T(1,128)S(1)} %bitcast.11, s32[2,192]{1,0:T(2,128)S(1)} %bitcast.10, s32[1,1]{1,0:T(1,128)S(6)} %copy.10.count_ref), custom_call_target="tpu_custom_call" | custom-call | tf_op jit(solution)/shard_map/sweeps/pallas_call | solution.py:465
  69.9 0.6 copy.11
  (1 shorter events, 0.0 us)
Async XLA Ops:
  0.7 0.7 copy-start.3
  1.3 0.7 copy-start.1
  1.3 0.7 copy-start.2
  2.0 0.8 %copy-start = (bf16[1,128,128]{2,1,0:T(8,128)(2,1)S(1)}, bf16[1,128,128]{2,1,0:T(8,128)(2,1)}, u32[]{:S(2)}) copy-start(bf16[1,128,128]{2,1,0:T(8,128)(2,1)} %param.5) | copy-start | bytes 98308

commit v4 on v3

--- a/solution.py
+++ b/solution.py
@@ -154,8 +154,8 @@
         ((0, 2), (0, 4), bottom, along(-2)),
         ((0, -2), (1, -2), full, across),
         ((0, 2), (1, 2), full, across),
-        ((0, -1), (1, -1), full, across),
-        ((0, 1), (1, 1), full, across),
+        ((1, 0), (1, -1), full, along(1)),
+        ((1, 0), (1, 1), full, along(-1)),
         ((1, -2), (1, -3), full, along(1)),
         ((1, 2), (1, 3), full, along(-1)),
         ((0, 4), (1, 4), full, across),
@@ -216,7 +216,7 @@
 
     for c, e, device in owners:
         put(place_of, (2 - c) * 2 + e, device)
-    pass_on(0, 0, 1, 2, 3, 4)
+    pass_on(0, 4, 2, 3, 0, 1)
 
     def spread(slot):
         turned = jnp.transpose(geo_in[slot, :, 0:FPD])
@@ -308,25 +308,40 @@
 
         lax.fori_loop(0, CYC, one, 0)
 
-    def partial_of(sweep, c, e, device):
+    def partial_of(sweep, part, c, e, device):
         index = (0, 1, None, 2, 3, 4)[(2 - c) * 2 + e]
+        sem = (sweep * 2 + part) * 5 + index
         return (
-            total.at[sweep, pl.ds((c * 2 + e) * FPD, FPD)],
-            part_in.at[sweep, index],
-            part_send.at[sweep * 5 + index],
-            part_recv.at[sweep * 5 + index],
+            total.at[sweep, pl.ds((c * 2 + e) * FPD + part * BS, BS)],
+            part_in.at[sweep, index, pl.ds(part * BS, BS)],
+            part_send.at[sem],
+            part_recv.at[sem],
             device,
         )
 
-    def exchange(sweep):
-        for owner in owners:
-            put(partial_of, sweep, *owner)
-        result = start + total[sweep, 2 * FPD : 3 * FPD, :]
-        for owner in owners:
-            copy(*partial_of(sweep, *owner)).wait_recv()
-        for index in range(5):
-            result = result + part_in[sweep, index]
-        return result
+    def exchange(sweep, take):
+        for part in range(2):
+            for owner in owners:
+                put(partial_of, sweep, part, *owner)
+        for part in range(2):
+            rows = slice(part * BS, (part + 1) * BS)
+            result = current[0, 0, rows, :]
+            result = result + total[sweep, 2 * FPD + part * BS : 2 * FPD + (part + 1) * BS, :]
+            for owner in owners:
+                copy(*partial_of(sweep, part, *owner)).wait_recv()
+            for index in range(5):
+                result = result + part_in[sweep, index, rows, :]
+            take(part, rows, result)
+
+    def sweep_on(part, rows, result):
+        current[1, 0, rows, :] = result
+        pass_on(1, *half(part, 4, 2, 3, 0, 1))
+
+    finals = []
+
+    def finish(part, rows, result):
+        finals.append(result)
+
 
     for slot in (0, 1, 3, 4, 5):
         spread(slot)
@@ -338,8 +353,9 @@
 
         @pl.when(slot == 2)
         def _():
+            arrive(0, 4)
+            pass_on(0, 11, 12)
             arrive(0, 2, 3)
-            pass_on(0, 11, 12)
 
         @pl.when(slot == 3)
         def _():
@@ -355,7 +371,6 @@
         @pl.when(slot == 6)
         def _():
             told(1, -1, 1)
-            arrive(0, 4)
 
         @pl.when(slot == 7)
         def _():
@@ -414,14 +429,11 @@
         @pl.when(n == 1)
         def _():
             for part in range(2):
+                arrive(1, *half(part, 4))
+                pass_on(1, *half(part, 11, 12))
+                arrive(1, *half(part, 2, 3))
                 arrive(1, *half(part, 0, 1))
                 pass_on(1, *half(part, 5, 6, 9, 10), *half(0, 7 + part), *half(1, 7 + part))
-                arrive(1, *half(part, 2, 3))
-                pass_on(1, *half(part, 11, 12))
-
-        @pl.when(n == 5)
-        def _():
-            arrive(1, *half(0, 4), *half(1, 4))
 
         @pl.when(n == 6)
         def _():
@@ -447,11 +459,10 @@
         add_swept(n)
         return 0
 
-    current[1, 0] = exchange(0)
-    for part in range(2):
-        pass_on(1, *half(part, 0, 1, 2, 3, 4))
+    exchange(0, sweep_on)
     lax.fori_loop(0, 2 * nz, swept_step, 0)
-    final = exchange(1)
+    exchange(1, finish)
+    final = jnp.concatenate(finals, axis=0)
     out_ref[...] = sum(dot(placed16, piece) for piece in split3(final))
 
     for place, which in sends:
@@ -484,8 +495,8 @@
             pltpu.SemaphoreType.DMA((2 * nz,)),
             pltpu.SemaphoreType.DMA((48,)),
             pltpu.SemaphoreType.DMA((48,)),
-            pltpu.SemaphoreType.DMA((10,)),
-            pltpu.SemaphoreType.DMA((10,)),
+            pltpu.SemaphoreType.DMA((20,)),
+            pltpu.SemaphoreType.DMA((20,)),
         ],
         compiler_params=pltpu.CompilerParams(
             collective_id=0, has_side_effects=True, vmem_limit_bytes=40 * 2**20

time: 70.7 us -> 69 us (0.976)
  Pallas kernels: 67.1 us -> 65.3 us
    pallas_call x1, Pallas kernels: 67.1 us -> 65.3 us  [per_device(): pl.pallas_call(functools.partial(kernel, nb, nz), out_shape=jax.ShapeDtyp...]
where the time goes in v4:
time: 69 us; the launch traced here: 68.8 us
  Pallas kernels  65.3 us (95%)
  local copies, waits for them, and re-layouts  2.75 us (4%)
    pallas_call x1, Pallas kernels, per_device(): pl.pallas_call(functools.partial(kernel, nb, nz), out_shape=jax.ShapeDtyp...  65.3 us
    unnamed x10, local copies, waits for them, and re-layouts  2.75 us

profile of v4, /device:TPU:1, one launch (start us, length us, event | category | flops | bytes accessed | tf_op | source)
XLA Modules:
  0.0 68.8 jit_solution(3325717797753244162)
XLA Ops:
  0.7 0.0 copy-start.3
  0.7 0.7 copy-done.3
  1.3 0.0 copy-start.1
  1.3 0.0 copy-start.2
  1.3 0.7 copy-done.1
  2.0 0.0 copy-done.2
  2.0 0.0 copy-start
  2.0 0.8 %copy-done = bf16[1,128,128]{2,1,0:T(8,128)(2,1)S(1)} copy-done((bf16[1,128,128]{2,1,0:T(8,128)(2,1)S(1)}, bf16[1,128,128]{2,1,0:T(8,128)(2,1)}, u32[]{:S(2)}) %copy-start) | copy-done | bytes 32792
  2.8 65.3 %sweeps.1 = f32[128,128]{1,0:T(8,128)S(1)} custom-call(bf16[128,128]{1,0:T(8,128)(2,1)S(1)} %bitcast.8, f32[6,128]{1,0:T(8,128)S(1)} %bitcast.9, s32[1,128]{1,0:T(1,128)S(1)} %bitcast.11, s32[2,192]{1,0:T(2,128)S(1)} %bitcast.10, s32[1,1]{1,0:T(1,128)S(6)} %copy.10.count_ref), custom_call_target="tpu_custom_call" | custom-call | tf_op jit(solution)/shard_map/sweeps/pallas_call | solution.py:476
  68.1 0.6 copy.11
  (1 shorter events, 0.0 us)
Async XLA Ops:
  0.7 0.7 copy-start.3
  1.3 0.7 copy-start.1
  1.3 0.7 copy-start.2
  2.0 0.8 %copy-start = (bf16[1,128,128]{2,1,0:T(8,128)(2,1)S(1)}, bf16[1,128,128]{2,1,0:T(8,128)(2,1)}, u32[]{:S(2)}) copy-start(bf16[1,128,128]{2,1,0:T(8,128)(2,1)} %param.5) | copy-start | bytes 98308

commit v5 on v4

--- a/solution.py
+++ b/solution.py
@@ -158,7 +158,8 @@
         ((1, 0), (1, 1), full, along(-1)),
         ((1, -2), (1, -3), full, along(1)),
         ((1, 2), (1, 3), full, along(-1)),
-        ((0, 4), (1, 4), full, across),
+        ((1, -2), (1, 4), top, along(2)),
+        ((1, 2), (1, 4), bottom, along(-2)),
     ]
 
     halves = []
@@ -380,7 +381,7 @@
         def _():
             told(1, -2, 2)
             arrive(0, 9, 10)
-            pass_on(0, 13, 14)
+            pass_on(0, 13, 14, 15, 16)
 
         @pl.when(slot == 9)
         def _():
@@ -389,7 +390,6 @@
         @pl.when(slot == 10)
         def _():
             arrive(0, 7, 8)
-            pass_on(0, 15)
 
         @pl.when(slot == 11)
         def _():
@@ -421,7 +421,7 @@
     visible(0)
     chunks(functools.partial(make_green, 0))
     lax.fori_loop(1, 2 * nz, start_step, 0)
-    arrive(0, 15)
+    arrive(0, 15, 16)
     weigh_start(slot_of(1, 4))
     chunks(functools.partial(add_start, slot_of(1, 4)))
 
@@ -439,9 +439,8 @@
         def _():
             for part in range(2):
                 arrive(1, *half(part, 9, 10))
-                pass_on(1, *half(part, 13, 14))
+                pass_on(1, *half(part, 13, 14), *half(0, 15 + part), *half(1, 15 + part))
             arrive(1, *half(0, 7, 8), *half(1, 7, 8))
-            pass_on(1, *half(0, 15), *half(1, 15))
             arrive(1, *half(0, 11, 12), *half(1, 11, 12))
 
         @pl.when(n == 10)
@@ -454,7 +453,7 @@
 
         @pl.when(n == 15)
         def _():
-            arrive(1, *half(0, 15), *half(1, 15))
+            arrive(1, *half(0, 15, 16), *half(1, 15, 16))
 
         add_swept(n)
         return 0
@@ -493,8 +492,8 @@
             pltpu.SemaphoreType.DMA((6,)),
             pltpu.SemaphoreType.DMA((2 * nz,)),
             pltpu.SemaphoreType.DMA((2 * nz,)),
-            pltpu.SemaphoreType.DMA((48,)),
-            pltpu.SemaphoreType.DMA((48,)),
+            pltpu.SemaphoreType.DMA((51,)),
+            pltpu.SemaphoreType.DMA((51,)),
             pltpu.SemaphoreType.DMA((20,)),
             pltpu.SemaphoreType.DMA((20,)),
         ],

time: 69 us -> 68.6 us (level)
  no operation moved by 1% of the time
where the time goes in v5:
time: 68.6 us; the launch traced here: 68.4 us
  Pallas kernels  65 us (95%)
  local copies, waits for them, and re-layouts  2.75 us (4%)
    pallas_call x1, Pallas kernels, per_device(): pl.pallas_call(functools.partial(kernel, nb, nz), out_shape=jax.ShapeDtyp...  65 us
    unnamed x10, local copies, waits for them, and re-layouts  2.75 us

profile of v5, /device:TPU:1, one launch (start us, length us, event | category | flops | bytes accessed | tf_op | source)
XLA Modules:
  0.0 68.4 jit_solution(2327108387056510114)
XLA Ops:
  0.7 0.0 copy-start.3
  0.7 0.7 copy-done.3
  1.3 0.0 copy-start.1
  1.3 0.0 copy-start.2
  1.3 0.7 copy-done.1
  2.0 0.0 copy-done.2
  2.0 0.0 copy-start
  2.0 0.8 %copy-done = bf16[1,128,128]{2,1,0:T(8,128)(2,1)S(1)} copy-done((bf16[1,128,128]{2,1,0:T(8,128)(2,1)S(1)}, bf16[1,128,128]{2,1,0:T(8,128)(2,1)}, u32[]{:S(2)}) %copy-start) | copy-done | bytes 32792
  2.8 65.0 %sweeps.1 = f32[128,128]{1,0:T(8,128)S(1)} custom-call(bf16[128,128]{1,0:T(8,128)(2,1)S(1)} %bitcast.8, f32[6,128]{1,0:T(8,128)S(1)} %bitcast.9, s32[1,128]{1,0:T(1,128)S(1)} %bitcast.11, s32[2,192]{1,0:T(2,128)S(1)} %bitcast.10, s32[1,1]{1,0:T(1,128)S(6)} %copy.10.count_ref), custom_call_target="tpu_custom_call" | custom-call | tf_op jit(solution)/shard_map/sweeps/pallas_call | solution.py:475
  67.8 0.6 copy.11
  (1 shorter events, 0.0 us)
Async XLA Ops:
  0.7 0.7 %copy-start.3 = (f32[1,6,128]{2,0,1:T(1,128)S(1)}, f32[1,6,128]{2,0,1:T(1,128)}, u32[]{:S(2)}) copy-start(f32[1,6,128]{2,0,1:T(1,128)} %param.6) | copy-start | bytes 9220
  1.3 0.7 copy-start.1
  1.3 0.7 copy-start.2
  2.0 0.8 %copy-start = (bf16[1,128,128]{2,1,0:T(8,128)(2,1)S(1)}, bf16[1,128,128]{2,1,0:T(8,128)(2,1)}, u32[]{:S(2)}) copy-start(bf16[1,128,128]{2,1,0:T(8,128)(2,1)} %param.5) | copy-start | bytes 98308
